TPU v7x, 256 devices: a whole 4x4x8 slice. The times are simulated.
256 devices in a mesh: pair: 64 (over z, y, core), vec: 4 (over x).
Axes of the slice: x: 4, y: 4, z: 8, core: 2. Of those that a mesh axis runs over, the one named last changes fastest.
Arguments:
- vectors: float32 [262144, 1536], P(('pair', 'vec')), may hold values from -1 to 1
- columns: float32 [2, 262144, 256], P(None, ('pair', 'vec')), may hold values from -6 to 6
- inverse_factor: float32 [2, 256, 256], replicated, as said below
- diagonal: float32 [262144], P(('pair', 'vec')), may hold values from 4 to 12
- pivots: int32 [2, 256], replicated, may hold values from 0 to 262143, as said below
- shell_map: int32 [262144], P(('pair', 'vec')), may hold values from 0 to 16383
Outputs:
- relaid: float32 [512, 262144], P(('pair', 'vec'))
- diagonal_out: float32 [262144], P(('pair', 'vec'))
- shell_sums: float32 [16384], P(('pair', 'vec'))
Inputs may be any that keep to these rules, and one draw needn't show every extreme that they name: The 256 pivots of batch b are different rows of one shard, the owner o_b: all within o_b * 1024 to (o_b + 1) * 1024 - 1; the two batches have different owners, one of which is the last shard; each batch includes its owner's last row. Each inverse_factor[b] is upper triangular with a positive diagonal.
All inputs are finite; a program needn't handle non-finite values.
Results may differ from a plain program's by a relative error of at most 0.00007.
Values sent between devices are 32-bit elements; how exact they have to be, the bound alone decides.
A program may use at most 64 MiB of HBM per device.

v0:
```python
import jax
import jax.numpy as jnp
from jax import lax
from jax.sharding import PartitionSpec as P

NSP_DEV = 64


def from_root(shard, axis, root):
    mine = lax.axis_index(axis) == root
    return lax.psum(jnp.where(mine, shard, jnp.zeros_like(shard)), axis)


def contract(left, right, left_dim, right_dim):
    return lax.dot_general(
        left,
        right,
        (((left_dim,), (right_dim,)), ((), ())),
        precision=lax.Precision.HIGHEST,
        preferred_element_type=jnp.float32,
    )


def on_device(vectors, columns, inverse_factor, diagonal, pivots, shell_map):
    rows_dev = vectors.shape[0]
    batch = inverse_factor.shape[1]
    npair = lax.axis_size("pair")
    nvec = lax.axis_size("vec")
    per_device = 2 * batch // (npair * nvec)
    factor_first = inverse_factor[0]
    factor_second = inverse_factor[1]
    owner_first = pivots[0, 0] // rows_dev
    owner_second = pivots[1, 0] // rows_dev
    local_first = pivots[0] - owner_first * rows_dev
    local_second = pivots[1] - owner_second * rows_dev
    picked_first = jnp.take(vectors, local_first, axis=0, mode="clip")
    rows_first = from_root(picked_first, ("pair", "vec"), owner_first)
    resid_first = columns[0] - contract(vectors, rows_first, 1, 1)
    new_first = contract(factor_first, resid_first, 0, 1)
    picked_new = jnp.take(new_first, local_second, axis=1, mode="clip").T
    picked_both = jnp.concatenate(
        [jnp.take(vectors, local_second, axis=0, mode="clip"), picked_new], axis=1
    )
    rows_both = from_root(picked_both, ("pair", "vec"), owner_second)
    rows_old = rows_both[:, : vectors.shape[1]]
    rows_new = rows_both[:, vectors.shape[1] :]
    resid_second = (
        columns[1] - contract(vectors, rows_old, 1, 1) - contract(new_first, rows_new, 0, 1)
    )
    new_second = contract(factor_second, resid_second, 0, 1)
    diagonal_out = (
        diagonal - jnp.sum(new_first * new_first, axis=0) - jnp.sum(new_second * new_second, axis=0)
    )
    stacked = jnp.concatenate([new_first, new_second], axis=0)
    arrived = lax.all_to_all(
        lax.all_to_all(stacked, "pair", split_axis=0, concat_axis=1, tiled=True),
        "vec",
        split_axis=0,
        concat_axis=1,
        tiled=True,
    )
    relaid = (
        arrived.reshape(per_device, nvec, npair, rows_dev)
        .transpose(0, 2, 1, 3)
        .reshape(per_device, nvec * npair * rows_dev)
    )
    shell_count = NSP_DEV * npair * nvec
    local_sums = jax.ops.segment_sum(diagonal_out, shell_map, num_segments=shell_count)
    shell_sums = lax.psum_scatter(local_sums, ("pair", "vec"), scatter_dimension=0, tiled=True)
    return (relaid, diagonal_out, shell_sums)


def solution(mesh):
    in_specs = (
        P(("pair", "vec"), None),
        P(None, ("pair", "vec"), None),
        P(),
        P(("pair", "vec")),
        P(),
        P(("pair", "vec")),
    )
    out_specs = (P(("pair", "vec"), None), P(("pair", "vec")), P(("pair", "vec")))
    return jax.shard_map(
        on_device, mesh=mesh, in_specs=in_specs, out_specs=out_specs, check_vma=False
    )
```

profile of v0, /device:TPU:1, one launch (start us, length us, event | category | flops | bytes accessed | tf_op | source)
XLA Modules:
  0.0 895.1 jit_solution(5074686159080829141)
XLA Ops:
  7.2 0.0 all-reduce.5.cloned.1.call-start
  7.2 1.3 fusion.18
  13.7 0.8 slice_subtract_fusion
  14.5 4.8 gather_fusion
  19.3 1.3 broadcast_select_fusion
  20.6 0.0 all-reduce.7.cloned.1.call-start
  20.6 1.7 fusion.17
  22.3 0.3 copy.30
  22.7 5.9 gather_fusion.1
  28.5 253.8 %all-reduce.5.cloned.1.call-done = f32[256,1536]{1,0:T(8,128)} async-done(((f32[256,1536]{1,0:T(8,128)}), f32[256,1536]{1,0:T(8,128)}) %all-reduce.5.cloned.1.call-update) | async-done | bytes 1572880 | tf_op jit(solution)/shard_map/psum | solution.py:11
  282.3 8.3 fusion.5
  290.6 1.1 multiply_reduce_fusion.1
  291.7 0.3 copy.22
  292.1 1.0 gather_fusion.2
  293.0 2.8 maximum_select_fusion
  295.8 0.3 copy.31
  296.2 258.8 %all-reduce.7.cloned.1.call-done = f32[256,1792]{1,0:T(8,128)} async-done(((f32[256,1792]{1,0:T(8,128)}), f32[256,1792]{1,0:T(8,128)}) %all-reduce.7.cloned.1.call-update) | async-done | bytes 1835024 | tf_op jit(solution)/shard_map/psum | solution.py:11
  555.0 8.3 fusion.6
  563.2 2.1 convolution_subtract_fusion
  565.4 1.1 multiply_reduce_fusion
  566.5 0.2 maximum_bitcast_fusion
  566.8 60.2 %all_to_all.32 = f32[64,8,1024]{2,1,0:T(8,128)S(1)} all-to-all(f32[64,8,1024]{2,1,0:T(8,128)S(1)} %maximum_bitcast_fusion), channel_id=1, replica_groups=mesh['pair'=64,'vec'=4] {'pair'}, dimensions={0} | all-to-all | bytes 4194304 | tf_op jit(solution)/shard_map/all_to_all | solution.py:56
  627.0 1.2 copy.24
  628.2 2.9 all_to_all.27
  631.1 3.7 all-to-all-start.1
  634.9 0.0 all-reduce.9.cloned.1.call-start
  635.0 6.6 scatter_custom_fusion
  641.6 236.4 %all-reduce.9.cloned.1.call-done = f32[16384]{0:T(1024)} async-done(((f32[16384]{0:T(1024)}), f32[16384]{0:T(1024)}) %all-reduce.9.cloned.1.call-update) | async-done | bytes 65552
  878.0 1.3 dynamic-slice
  879.2 2.9 reshape.82
  882.2 2.9 copy.26
  885.1 3.5 reshape.45
  (15 shorter events, 0.1 us)
Async XLA Ops:
  7.2 275.1 %all-reduce.5.cloned.1.call-start = ((), (), s32[]{:S(2)}) async-start(), calls=%async_computation.2 | async-start | bytes 3145728 | tf_op jit(solution)/shard_map/psum | solution.py:11
  20.6 534.4 %all-reduce.7.cloned.1.call-start = ((), (), s32[]{:S(2)}) async-start(), calls=%async_computation.3 | async-start | bytes 3670016 | tf_op jit(solution)/shard_map/psum | solution.py:11
  28.5 262.0 %copy-start = (f32[2,256,256]{2,1,0:T(8,128)S(1)}, f32[2,256,256]{2,1,0:T(8,128)}, u32[]{:S(2)}) copy-start(f32[2,256,256]{2,1,0:T(8,128)} %param.8) | copy-start | bytes 1572868
  563.2 2.1 copy-start.1
  631.1 3.8 copy-start.2
  631.1 248.1 %all-to-all-start.1 = ((f32[4,2,65536]{2,1,0:T(2,128)}), f32[4,2,65536]{2,1,0:T(2,128)S(1)}, u32[]{:S(2)}, u32[]{:S(2)}) async-start(f32[4,2,65536]{2,1,0:T(2,128)} %all_to_all.27), calls=%async_computation.1 | async-start | bytes 4194304 | tf_op jit(solution)/shard_map/all_to_all | solution.py:55
  634.9 243.1 %all-reduce.9.cloned.1.call-start = ((), (), s32[]{:S(2)}) async-start(), calls=%async_computation.4 | async-start | bytes 131072
  634.9 247.3 %copy-start.3 = (f32[1024]{0:T(1024)}, f32[1024]{0:T(1024)S(1)}, u32[]{:S(2)}) copy-start(f32[1024]{0:T(1024)S(1)} %subtract_subtract_fusion) | copy-start | bytes 12292
Sparse Core Ops, SparseCore 0:
  20.7 261.5 all-reduce.4
  296.0 258.9 all-reduce.6
  641.7 236.1 all-reduce.8
where the time goes:
time: 896 us; the launch traced here: 895 us
  waiting for transfers between devices  749 us (84%)
  blocking collectives  60.2 us (7%)
  local copies, waits for them, and re-layouts  30.4 us (3%)
  matrix products  20.9 us (2%)
  between operations  19.1 us (2%)
  other arithmetic  11.7 us (1%)
    psum x2, waiting for transfers between devices, from_root(): return lax.psum(jnp.where(mine, shard, jnp.zeros_like(shard)), axis)  513 us
    unnamed x4, waiting for transfers between devices  236 us
    all_to_all x1, blocking collectives, on_device(): lax.all_to_all(stacked, 'pair', split_axis=0, concat_axis=1, tiled=True)  60.2 us
    dot_general x5, matrix products, contract(): lax.dot_general(left, right, (((left_dim,), (right_dim,)), ((), ())), pre...  20.9 us
  transfers between devices with their start and end apart: 4, of which 3 were waited for; matrix products, arithmetic and copies ran while one was open for 2% of the time, Pallas kernels for 0%

commit v1 on v0

--- a/solution.py
+++ b/solution.py
@@ -1,6 +1,10 @@
+import functools
+
 import jax
 import jax.numpy as jnp
 from jax import lax
+from jax.experimental import pallas as pl
+from jax.experimental.pallas import tpu as pltpu
 from jax.sharding import PartitionSpec as P
 
 NSP_DEV = 64
@@ -19,6 +23,48 @@
         precision=lax.Precision.HIGHEST,
         preferred_element_type=jnp.float32,
     )
+
+
+def exchange_kernel(npair, nvec, new_ref, out_ref, send_sem, recv_sem):
+    pair = lax.axis_index("pair")
+    vec = lax.axis_index("vec")
+    devices, _, rows = new_ref.shape
+    me = pair * nvec + vec
+    here = out_ref.at[:, pl.ds(pl.multiple_of(me * rows, rows), rows)]
+    pltpu.make_async_copy(new_ref.at[me], here, recv_sem).start()
+
+    def send(step, carry):
+        to_pair = lax.rem(pair + lax.rem(step, 8) * 8 + lax.div(lax.rem(step, 64), 8), npair)
+        to_vec = lax.rem(vec + lax.div(step, 64), nvec)
+        pltpu.make_async_remote_copy(
+            src_ref=new_ref.at[to_pair * nvec + to_vec],
+            dst_ref=here,
+            send_sem=send_sem,
+            recv_sem=recv_sem,
+            device_id=(to_pair, to_vec),
+            device_id_type=pl.DeviceIdType.MESH,
+        ).start()
+        return carry
+
+    lax.fori_loop(1, devices, send, 0)
+    pltpu.make_async_copy(out_ref, out_ref, recv_sem).wait()
+    sent = new_ref.at[pl.ds(0, devices - 1)]
+    pltpu.make_async_copy(sent, sent, send_sem).wait()
+
+
+def exchange(new):
+    npair = lax.axis_size("pair")
+    nvec = lax.axis_size("vec")
+    devices, per_device, rows = new.shape
+    return pl.pallas_call(
+        functools.partial(exchange_kernel, npair, nvec),
+        out_shape=jax.ShapeDtypeStruct((per_device, devices * rows), jnp.float32),
+        in_specs=[pl.BlockSpec(memory_space=pl.ANY)],
+        out_specs=pl.BlockSpec(memory_space=pl.ANY),
+        scratch_shapes=[pltpu.SemaphoreType.DMA, pltpu.SemaphoreType.DMA],
+        compiler_params=pltpu.CompilerParams(has_side_effects=True),
+        name="exchange",
+    )(new)
 
 
 def on_device(vectors, columns, inverse_factor, diagonal, pivots, shell_map):
@@ -52,18 +98,7 @@
         diagonal - jnp.sum(new_first * new_first, axis=0) - jnp.sum(new_second * new_second, axis=0)
     )
     stacked = jnp.concatenate([new_first, new_second], axis=0)
-    arrived = lax.all_to_all(
-        lax.all_to_all(stacked, "pair", split_axis=0, concat_axis=1, tiled=True),
-        "vec",
-        split_axis=0,
-        concat_axis=1,
-        tiled=True,
-    )
-    relaid = (
-        arrived.reshape(per_device, nvec, npair, rows_dev)
-        .transpose(0, 2, 1, 3)
-        .reshape(per_device, nvec * npair * rows_dev)
-    )
+    relaid = exchange(stacked.reshape(npair * nvec, per_device, rows_dev))
     shell_count = NSP_DEV * npair * nvec
     local_sums = jax.ops.segment_sum(diagonal_out, shell_map, num_segments=shell_count)
     shell_sums = lax.psum_scatter(local_sums, ("pair", "vec"), scatter_dimension=0, tiled=True)

time: 896 us -> 831 us (0.927)
  Pallas kernels: 0 us -> 65.1 us
  blocking collectives: 60.2 us -> 0 us
  waiting for transfers between devices: 749 us -> 692 us
  local copies, waits for them, and re-layouts: 30.4 us -> 19.5 us
    pallas_call x0 -> x1, Pallas kernels: none -> 65.1 us  [exchange(): pl.pallas_call(functools.partial(exchange_kernel, npair, nvec), out_shape...]
    all_to_all x1 -> x0, blocking collectives: 60.2 us -> none  [on_device(): lax.all_to_all(stacked, 'pair', split_axis=0, concat_axis=1, tiled=True)]
    unnamed x4, waiting for transfers between devices: 236 us -> 178 us
  transfers between devices with their start and end apart: 4 -> 3, of which waited for: 3 -> 3; matrix products, arithmetic and copies ran while one was open for 2% -> 1% of each run, Pallas kernels for 0% -> 8%
where the time goes in v1:
time: 831 us
  waiting for transfers between devices  692 us (83%)
  Pallas kernels  65.1 us (8%)
  matrix products  21.5 us (3%)
  local copies, waits for them, and re-layouts  19.5 us (2%)
  between operations  19.1 us (2%)
  other arithmetic  13 us (2%)
    psum x2, waiting for transfers between devices, from_root(): return lax.psum(jnp.where(mine, shard, jnp.zeros_like(shard)), axis)  515 us
    unnamed x4, waiting for transfers between devices  178 us
    pallas_call x1, Pallas kernels, exchange(): pl.pallas_call(functools.partial(exchange_kernel, npair, nvec), out_shape...  65.1 us
    dot_general x5, matrix products, contract(): lax.dot_general(left, right, (((left_dim,), (right_dim,)), ((), ())), pre...  21.5 us
  transfers between devices with their start and end apart: 3, of which 3 were waited for; matrix products, arithmetic and copies ran while one was open for 1% of the time, Pallas kernels for 8%

profile of v1, /device:TPU:1, one launch (start us, length us, event | category | flops | bytes accessed | tf_op | source)
XLA Modules:
  0.0 830.8 jit_solution(8597125997959672131)
XLA Ops:
  7.2 0.0 all-reduce.5.cloned.1.call-start
  7.2 1.3 fusion.17
  13.7 0.8 slice_subtract_fusion
  14.5 4.8 gather_fusion
  19.3 1.3 broadcast_select_fusion
  20.5 0.0 all-reduce.5.cloned.1.call-update
  20.6 0.0 all-reduce.7.cloned.1.call-start
  20.6 0.0 copy-start
  20.6 6.0 gather_fusion.1
  26.7 255.6 %all-reduce.5.cloned.1.call-done = f32[256,1536]{1,0:T(8,128)} async-done(((f32[256,1536]{1,0:T(8,128)}), f32[256,1536]{1,0:T(8,128)}) %all-reduce.5.cloned.1.call-update) | async-done | bytes 1572880 | tf_op jit(solution)/shard_map/psum | solution.py:15
  282.3 7.7 fusion.5
  290.1 1.1 multiply_reduce_fusion.1
  291.2 0.3 copy.10
  291.5 1.0 gather_fusion.2
  292.5 0.0 copy-start.1
  292.5 2.9 maximum_select_fusion
  295.4 0.0 all-reduce.7.cloned.1.call-update
  295.5 0.2 all-reduce.9.cloned.1.call-start
  295.7 258.9 %all-reduce.7.cloned.1.call-done = f32[256,1792]{1,0:T(8,128)} async-done(((f32[256,1792]{1,0:T(8,128)}), f32[256,1792]{1,0:T(8,128)}) %all-reduce.7.cloned.1.call-update) | async-done | bytes 1835024 | tf_op jit(solution)/shard_map/psum | solution.py:15
  554.6 7.7 fusion.6
  562.3 0.0 copy-start.3
  562.4 2.8 convolution_subtract_fusion
  565.2 0.0 copy-start.4
  565.2 2.1 multiply_reduce_fusion
  567.3 6.6 scatter_custom_fusion
  573.9 0.0 all-reduce.9.cloned.1.call-update
  574.0 1.4 pad_maximum_fusion
  575.4 2.2 reshape.33.new_ref
  577.6 65.1 %exchange.1 = f32[2,262144]{1,0:T(2,128)} custom-call(f32[256,2,1024]{2,1,0:T(2,128)} %reshape.33.new_ref), custom_call_target="tpu_custom_call" | custom-call | tf_op jit(solution)/shard_map/exchange/pallas_call | solution.py:59
  642.7 177.7 %all-reduce.9.cloned.1.call-done = f32[16384]{0:T(1024)} async-done(((f32[16384]{0:T(1024)}), f32[16384]{0:T(1024)}) %all-reduce.9.cloned.1.call-update) | async-done | bytes 65552
  820.4 1.3 dynamic-slice
  821.7 2.6 copy.15
  (11 shorter events, 0.0 us)
Async XLA Ops:
  7.2 275.1 %all-reduce.5.cloned.1.call-start = ((), (), s32[]{:S(2)}) async-start(), calls=%async_computation | async-start | bytes 3145728 | tf_op jit(solution)/shard_map/psum | solution.py:15
  20.6 534.0 %all-reduce.7.cloned.1.call-start = ((), (), s32[]{:S(2)}) async-start(), calls=%async_computation.1 | async-start | bytes 3670016 | tf_op jit(solution)/shard_map/psum | solution.py:15
  20.6 261.7 %copy-start = (f32[2,1024,256]{2,1,0:T(8,128)S(1)}, f32[2,1024,256]{2,1,0:T(8,128)}, u32[]{:S(2)}) copy-start(f32[2,1024,256]{2,1,0:T(8,128)} %param.7) | copy-start | bytes 6291460
  26.7 263.4 %copy-start.2 = (f32[2,256,256]{2,1,0:T(8,128)S(1)}, f32[2,256,256]{2,1,0:T(8,128)}, u32[]{:S(2)}) copy-start(f32[2,256,256]{2,1,0:T(8,128)} %param.8) | copy-start | bytes 1572868
  292.5 262.1 %copy-start.1 = (f32[2,1024,256]{2,1,0:T(8,128)S(1)}, f32[2,1024,256]{2,1,0:T(8,128)}, u32[]{:S(2)}) copy-start(f32[2,1024,256]{2,1,0:T(8,128)} %param.7) | copy-start | bytes 6291460
  295.5 525.0 %all-reduce.9.cloned.1.call-start = ((), (), s32[]{:S(2)}) async-start(), calls=%async_computation.2 | async-start | bytes 131072
  562.3 2.9 copy-start.3
  565.2 2.1 copy-start.4
  567.3 8.1 copy-start.5
Sparse Core Ops, SparseCore 0:
  20.7 261.5 all-reduce.4
  295.6 258.9 all-reduce.6
  574.1 246.2 all-reduce.8

commit v2 on v0

v2 whole, which is shorter than its diff:
```python
import functools

import jax
import jax.numpy as jnp
from jax import lax
from jax.experimental import pallas as pl
from jax.experimental.pallas import tpu as pltpu
from jax.sharding import PartitionSpec as P

F32 = jnp.float32
BF16 = jnp.bfloat16
MESH = pl.DeviceIdType.MESH

NZ, NY, NX, NC = 8, 4, 4, 2
BATCH = 256
RANK = 1536
ROWS = 1024
DEVICES = NZ * NY * NX * NC
SHELLS = 64
BLOCK = 512

LOW = (0, 512, 128)
HIGH = (1024, 384, 128)
WIDE = RANK + BATCH
LAST = (0, 768, 1536)


def split(x):
    high = x.astype(BF16)
    return high, (x - high.astype(F32)).astype(BF16)


def dot_nn(a, b):
    return lax.dot_general(a, b, (((1,), (0,)), ((), ())), preferred_element_type=F32)


def dot_nt(a, b):
    return lax.dot_general(a, b, (((1,), (1,)), ((), ())), preferred_element_type=F32)


def three(dot, a, b):
    return dot(a[0], b[0]) + (dot(a[0], b[1]) + dot(a[1], b[0]))


def times(i, n):
    return pl.multiple_of(i * n, n)


class Group:
    def __init__(self, spec, refs):
        self.first, self.width, self.part = spec
        (self.r0, self.h, self.r1a, self.r1b, self.h2a, self.h2b, self.r2a, self.r2b,
         self.g, self.r3, self.g2, self.send, self.recv) = refs


def group_scratch(spec):
    _, width, part = spec
    return [
        pltpu.VMEM((BATCH, width), F32),
        pltpu.VMEM((BATCH, width), F32),
        pltpu.VMEM((3, 32, width), F32),
        pltpu.VMEM((3, 32, width), F32),
        pltpu.VMEM((32, width), F32),
        pltpu.VMEM((32, width), F32),
        pltpu.VMEM((3, 8, width), F32),
        pltpu.VMEM((3, 8, width), F32),
        pltpu.VMEM((8, 2 * width), F32),
        pltpu.VMEM((NZ - 1, 8, part), F32),
        pltpu.VMEM((8, 2 * width), F32),
        pltpu.SemaphoreType.DMA((12,)),
        pltpu.SemaphoreType.DMA((16,)),
    ]


def last_scratch(spec):
    _, width, _ = spec
    return [
        pltpu.VMEM((8, 2 * width), F32),
        pltpu.SemaphoreType.DMA((12,)),
        pltpu.SemaphoreType.DMA((16,)),
    ]


def kernel(
    vectors, columns, factor, diagonal, pivots, shells,
    relaid, diagonal_out, sums_out,
    v32, vh, vl, c32, pick, pick_last, pa, pb, pah, pal, pbh, pbl, ya, yb,
    new, sums, arrived, load_sem, exchange_send, exchange_recv, sums_send, sums_recv,
    *group_refs,
):
    pair = lax.axis_index("pair")
    x = lax.axis_index("vec")
    z, y, c = pair // (NY * NC), (pair // NC) % NY, pair % NC
    me = pair * NX + x
    n = len(group_scratch(LOW))
    low, high = Group(LOW, group_refs[:n]), Group(HIGH, group_refs[n : 2 * n])
    g2_last, last_send, last_recv = group_refs[2 * n :]

    def at(z=z, y=y, x=x, c=c):
        return ((z * NY + y) * NC + c, x)

    def along_x(d):
        return (x + d) % NX

    def along_y(d):
        return (y + d) % NY

    def along_z(d):
        return (z + d) % NZ

    def push(src, dst, send_sem, recv_sem, device):
        pltpu.make_async_remote_copy(
            src_ref=src, dst_ref=dst, send_sem=send_sem, recv_sem=recv_sem,
            device_id=device, device_id_type=MESH,
        ).start()

    def take(ref, sem):
        pltpu.make_async_copy(ref, ref, sem).wait()

    def load(i, width=256):
        at_cols = pl.ds(times(i, width), width)
        return pltpu.make_async_copy(vectors.at[:, at_cols], v32.at[:, at_cols], load_sem.at[i])

    order = [(1 - c) * 2, (1 - c) * 2 + 1, c * 2, c * 2 + 1, 4, 5]
    for i in order:
        load(i).start()
    load_columns = pltpu.make_async_copy(columns, c32, load_sem.at[6])
    load_columns.start()

    barrier = pltpu.get_barrier_semaphore()

    def greet(device):
        pl.semaphore_signal(barrier, inc=1, device_id=device, device_id_type=MESH)

    greet(at(c=1 - c))
    for d in range(1, 4):
        greet(at(x=along_x(d)))
        greet(at(y=along_y(d)))
    for d in range(1, NZ):
        greet(at(z=along_z(d)))
    root = me == DEVICES - 1
    apart = (x != NX - 1).astype(jnp.int32) + (y != NY - 1).astype(jnp.int32) + (c != NC - 1).astype(jnp.int32)

    @pl.when((z == NZ - 1) & (apart >= 2))
    def _():
        greet(at(z=NZ - 1, y=NY - 1, x=NX - 1, c=NC - 1))

    eye = lax.broadcasted_iota(jnp.int32, (BATCH, BATCH), 0) == lax.broadcasted_iota(jnp.int32, (BATCH, BATCH), 1)
    row = lax.broadcasted_iota(jnp.int32, (BATCH, ROWS), 1) + me * ROWS
    hot = [
        row == jnp.sum(jnp.where(eye, pivots[b : b + 1, :], 0), axis=1, keepdims=True)
        for b in range(2)
    ]
    hot_second = jnp.where(hot[1], 1.0, 0.0).astype(BF16)
    hot_any = jnp.where(hot[0] | hot[1], 1.0, 0.0).astype(BF16)
    kept = jnp.where(root, 0.0, 1.0).astype(F32)

    def gather(i):
        at_cols = pl.ds(times(i, 256), 256)
        load(i).wait()
        vh[:, at_cols], vl[:, at_cols] = split(v32[:, at_cols])
        rows = dot_nn(hot_any, vh[:, at_cols]) + dot_nn(hot_any, vl[:, at_cols])
        pick_last[:, at_cols] = rows
        pick[:, at_cols] = rows * kept

    def half(first, width, core):
        return pl.ds(pl.multiple_of(first + core * width, 128), width)

    def spread(p, g2, first, width, send, recv):
        mine = half(first, width, c)
        rows_a = pl.ds(times(x * NY + y, 8), 8)
        rows_b = pl.ds(pl.multiple_of(128 + (y * NX + x) * 8, 8), 8)
        p[rows_a, mine] = g2[:, :width]
        p[rows_b, mine] = g2[:, width:]
        for d in range(1, 4):
            push(g2.at[:, pl.ds(0, width)], p.at[rows_a, mine], send.at[6], recv.at[6], at(y=along_y(d)))
            push(g2.at[:, pl.ds(width, width)], p.at[rows_b, mine], send.at[6], recv.at[7], at(x=along_x(d)))
        yield
        three_rows = p.at[pl.ds(0, 24), pl.ds(0, width)]
        block_a = p.at[pl.ds(times(x, 32), 32), mine]
        block_b = p.at[pl.ds(pl.multiple_of(128 + y * 32, 32), 32), mine]
        take(three_rows, recv.at[6])
        for d in range(1, 4):
            push(block_a, block_a, send.at[7], recv.at[7 + d], at(x=along_x(d)))
        push(block_a, block_a, send.at[8], recv.at[14], at(c=1 - c))
        take(three_rows, recv.at[7])
        for d in range(1, 4):
            push(block_b, block_b, send.at[7], recv.at[10 + d], at(y=along_y(d)))
        push(block_b, block_b, send.at[8], recv.at[14], at(c=1 - c))
        yield
        for d in range(1, 4):
            block = p.at[pl.ds(times(along_x(4 - d), 32), 32), mine]
            take(block, recv.at[7 + d])
            push(block, block, send.at[8], recv.at[14], at(c=1 - c))
            block = p.at[pl.ds(pl.multiple_of(128 + along_y(4 - d) * 32, 32), 32), mine]
            take(block, recv.at[10 + d])
            push(block, block, send.at[8], recv.at[14], at(c=1 - c))
        yield
        take(p.at[:, pl.ds(0, width)], recv.at[14])

    def spread_sent(p, width, send):
        take(p.at[pl.ds(0, 48), pl.ds(0, width)], send.at[6])
        take(p.at[pl.ds(0, 192), pl.ds(0, width)], send.at[7])
        take(p.at[:, pl.ds(0, width)], send.at[8])

    def reduce(s):
        width, part, send, recv = s.width, s.part, s.send, s.recv
        parts = 2 * width // part
        push(pick.at[:, half(s.first, width, 1 - c)], s.r0, send.at[0], recv.at[0], at(c=1 - c))
        yield
        take(s.r0, recv.at[0])
        s.h[...] = pick[:, half(s.first, width, c)] + s.r0[...]
        for d in range(1, 4):
            to = along_x(d)
            push(s.h.at[pl.ds(times(to, 32), 32)], s.r1a.at[d - 1], send.at[1], recv.at[1], at(x=to))
            to = along_y(d)
            push(s.h.at[pl.ds(pl.multiple_of(128 + to * 32, 32), 32)], s.r1b.at[d - 1], send.at[1], recv.at[2], at(y=to))
        yield
        take(s.r1a, recv.at[1])
        s.h2a[...] = (s.h[pl.ds(times(x, 32), 32), :] + s.r1a[0]) + (s.r1a[1] + s.r1a[2])
        for d in range(1, 4):
            to = along_y(d)
            push(s.h2a.at[pl.ds(times(to, 8), 8)], s.r2a.at[d - 1], send.at[2], recv.at[3], at(y=to))
        take(s.r1b, recv.at[2])
        s.h2b[...] = (s.h[pl.ds(pl.multiple_of(128 + y * 32, 32), 32), :] + s.r1b[0]) + (s.r1b[1] + s.r1b[2])
        for d in range(1, 4):
            to = along_x(d)
            push(s.h2b.at[pl.ds(times(to, 8), 8)], s.r2b.at[d - 1], send.at[2], recv.at[4], at(x=to))
        yield
        take(s.r2a, recv.at[3])
        s.g[:, :width] = (s.h2a[pl.ds(times(y, 8), 8), :] + s.r2a[0]) + (s.r2a[1] + s.r2a[2])
        take(s.r2b, recv.at[4])
        s.g[:, width:] = (s.h2b[pl.ds(times(x, 8), 8), :] + s.r2b[0]) + (s.r2b[1] + s.r2b[2])
        for d in range(1, NZ):
            to = along_z(d)

            @pl.when(to < parts)
            def _():
                push(s.g.at[:, pl.ds(times(to, part), part)], s.r3.at[d - 1], send.at[3], recv.at[5], at(z=to))

        yield
        mine = pl.ds(times(z, part), part)

        @pl.when(z < parts)
        def _():
            take(s.r3, recv.at[5])
            total = s.g[:, mine]
            for d in range(1, NZ):
                total = total + s.r3[d - 1]
            s.g2[:, mine] = total
            for d in range(1, NZ):
                push(s.g2.at[:, mine], s.g2.at[:, mine], send.at[4], recv.at[15], at(z=along_z(d)))

        yield

        @pl.when(z < parts)
        def _():
            take(s.g2.at[:, pl.ds(0, (parts - 1) * part)], recv.at[15])

        @pl.when(z >= parts)
        def _():
            take(s.g2.at[:, pl.ds(0, parts * part)], recv.at[15])

        yield from spread(pa, s.g2, s.first, width, send, recv)

    def reduce_sent(s):
        width, part, send = s.width, s.part, s.send
        parts = 2 * width // part
        take(s.r0, send.at[0])
        take(s.h.at[pl.ds(0, 192)], send.at[1])
        take(s.h.at[pl.ds(0, 48)], send.at[2])

        @pl.when(z < parts)
        def _():
            take(s.g2.at[:, pl.ds(0, (parts - 1) * part)], send.at[3])
            take(s.r3, send.at[4])

        @pl.when(z >= parts)
        def _():
            take(s.g2.at[:, pl.ds(0, parts * part)], send.at[3])

        spread_sent(pa, width, send)

    def from_last():
        first, width, _ = LAST

        @pl.when(root)
        def _():
            def rows_of(y, x, c):
                cols = half(first, width, c)
                return (
                    pick_last.at[pl.ds(times(x * NY + y, 8), 8), cols],
                    pick_last.at[pl.ds(pl.multiple_of(128 + (y * NX + x) * 8, 8), 8), cols],
                )

            for part, src in enumerate(rows_of(y, x, c)):
                g2_last[:, part * width : (part + 1) * width] = src[...]

            def send_to(k, carry):
                y_to, x_to, c_to = (y + k // 2) % NY, (x + k // 8) % NX, (c + k) % NC
                for part, src in enumerate(rows_of(y_to, x_to, c_to)):
                    push(src, g2_last.at[:, pl.ds(part * width, width)], last_send.at[0], last_recv.at[0],
                         at(y=y_to, x=x_to, c=c_to))
                return carry

            lax.fori_loop(1, NY * NX * NC, send_to, 0)

        yield

        @pl.when((z == NZ - 1) & jnp.logical_not(root))
        def _():
            take(g2_last, last_recv.at[0])

        @pl.when(z == NZ - 1)
        def _():
            for d in range(1, NZ):
                push(g2_last, g2_last, last_send.at[1], last_recv.at[1], at(z=along_z(d)))

        yield

        @pl.when(z != NZ - 1)
        def _():
            take(g2_last, last_recv.at[1])

        yield from spread(pb, g2_last, first, width, last_send, last_recv)

    def from_last_sent():
        _, width, _ = LAST

        @pl.when(root)
        def _():
            take(pick_last.at[pl.ds(0, 248)], last_send.at[0])

        @pl.when(z == NZ - 1)
        def _():
            take(pick_last.at[pl.ds(0, 56)], last_send.at[1])

        spread_sent(pb, width, last_send)

    for i in order[:4]:
        gather(i)

    @pl.when(root)
    def _():
        pl.semaphore_wait(barrier, 38)

    @pl.when(jnp.logical_not(root))
    def _():
        pl.semaphore_wait(barrier, 14)

    a, b, last = reduce(low), reduce(high), from_last()

    def go(*streams):
        for stream in streams:
            next(stream, None)

    go(a)
    gather(order[4])
    gather(order[5])
    load_columns.wait()
    own = split(c32[0])
    pick[:, RANK:] = dot_nn(hot_second, own[0]) + dot_nn(hot_second, own[1])
    go(b, last)
    go(a, b, a, b, last, a, b, last, a, b, last, a, b, last, a, b, last)

    pbh[...], pbl[...] = split(pb[...])

    def times_last(i, carry):
        rows = pl.ds(times(i, 256), 256)
        yb[rows, :] = three(dot_nt, (vh[rows, :], vl[rows, :]), (pbh[...], pbl[...]))
        return carry

    lax.fori_loop(0, ROWS // 256, times_last, 0)
    go(a, b, a, b)

    f0, f1 = factor[0], factor[1]
    pah[...], pal[...] = split(pa[:, :RANK])
    cross = three(dot_nt, (pah[...], pal[...]), (pbh[...], pbl[...]))
    last_first = jnp.broadcast_to(pivots[0:1, 0:1], (BATCH, BATCH)) >= (DEVICES - 1) * ROWS
    cross = jnp.where(last_first, cross, cross.T)
    f0_parts = split(f0)
    pivot_new = three(dot_nn, split(pa[:, RANK:] - cross), f0_parts)
    onto = split(three(dot_nt, f0_parts, split(pivot_new)))
    f0_t, f1_t = split(f0.T), split(f1.T)
    last_first = jnp.broadcast_to(pivots[0:1, 0:1], (BLOCK, BATCH)) >= (DEVICES - 1) * ROWS

    def times_other(i, carry):
        rows = pl.ds(times(i, 256), 256)
        ya[rows, :] = three(dot_nt, (vh[rows, :], vl[rows, :]), (pah[...], pal[...]))
        return carry

    lax.fori_loop(0, ROWS // 256, times_other, 0)

    kinds = DEVICES // 2
    for block in range(ROWS // BLOCK):
        rows = pl.ds(block * BLOCK, BLOCK)
        y_a, y_b = ya[rows, :], yb[rows, :]
        resid = c32[0, rows, :] - jnp.where(last_first, y_b, y_a)
        parts = split(resid)
        new_first = three(dot_nt, f0_t, parts)
        resid = c32[1, rows, :] - jnp.where(last_first, y_a, y_b) - three(dot_nn, parts, onto)
        new_second = three(dot_nt, f1_t, split(resid))
        new[:kinds, :, rows] = new_first.reshape(kinds, 2, BLOCK)
        new[kinds:, :, rows] = new_second.reshape(kinds, 2, BLOCK)
        diagonal_out[:, rows] = diagonal[:, rows] - jnp.sum(
            new_first * new_first + new_second * new_second, axis=0, keepdims=True
        )
        here = relaid.at[:, pl.ds(pl.multiple_of(me * ROWS + block * BLOCK, BLOCK), BLOCK)]

        def send_new(k, carry):
            y_to, x_to, c_to = (y + k // 4) % NY, (x + k // 16) % NX, (c + k // 64) % NC
            for batch in range(2):
                z_to = batch * (NZ // 2) + (z + k) % (NZ // 2)
                pair_to, x_to = at(z=z_to, y=y_to, x=x_to, c=c_to)
                to = pair_to * NX + x_to
                src = new.at[to, :, rows]

                @pl.when(to == me)
                def _():
                    pltpu.make_async_copy(src, here, exchange_recv).start()

                @pl.when(to != me)
                def _():
                    push(src, here, exchange_send, exchange_recv, (pair_to, x_to))

            return carry

        lax.fori_loop(0, kinds, send_new, 0)

    shell = shells[...]
    hot_device = jnp.where(
        lax.broadcasted_iota(jnp.int32, (DEVICES, ROWS), 0) == shell // SHELLS, 1.0, 0.0
    ).astype(BF16)
    values = jnp.where(
        lax.broadcasted_iota(jnp.int32, (128, ROWS), 0) == shell % SHELLS, diagonal_out[...], 0.0
    )
    first, rest = values.astype(BF16), values
    rest = rest - first.astype(F32)
    second, third = split(rest)
    total = dot_nt(hot_device, first) + (dot_nt(hot_device, second) + dot_nt(hot_device, third))
    sums[...] = total.reshape(DEVICES, 1, 128)
    pltpu.make_async_copy(sums.at[me], arrived.at[me], sums_recv).start()

    def send_sums(k, carry):
        z_to, y_to, x_to, c_to = along_z(k), (y + k // 8) % NY, (x + k // 32) % NX, (c + k // 128) % NC
        pair_to, x_to = at(z=z_to, y=y_to, x=x_to, c=c_to)
        push(sums.at[pair_to * NX + x_to], arrived.at[me], sums_send, sums_recv, (pair_to, x_to))
        return carry

    lax.fori_loop(1, DEVICES, send_sums, 0)

    reduce_sent(low)
    reduce_sent(high)
    from_last_sent()
    take(arrived, sums_recv)
    sums_out[...] = jnp.sum(arrived[...], axis=0)
    take(relaid, exchange_recv)
    take(new.at[pl.ds(0, DEVICES - 1)], exchange_send)
    take(sums.at[pl.ds(0, DEVICES - 1)], sums_send)


def on_device(vectors, columns, inverse_factor, diagonal, pivots, shell_map):
    vmem = pl.BlockSpec(memory_space=pltpu.VMEM)
    hbm = pl.BlockSpec(memory_space=pl.ANY)
    dma = pltpu.SemaphoreType.DMA
    relaid, diagonal_out, sums = pl.pallas_call(
        kernel,
        out_shape=[
            jax.ShapeDtypeStruct((2, ROWS * DEVICES), F32),
            jax.ShapeDtypeStruct((1, ROWS), F32),
            jax.ShapeDtypeStruct((1, 128), F32),
        ],
        in_specs=[hbm, hbm, vmem, vmem, vmem, vmem],
        out_specs=[hbm, vmem, vmem],
        scratch_shapes=[
            pltpu.VMEM((ROWS, RANK), F32),
            pltpu.VMEM((ROWS, RANK), BF16),
            pltpu.VMEM((ROWS, RANK), BF16),
            pltpu.VMEM((2, ROWS, BATCH), F32),
            pltpu.VMEM((BATCH, WIDE), F32),
            pltpu.VMEM((BATCH, RANK), F32),
            pltpu.VMEM((BATCH, WIDE), F32),
            pltpu.VMEM((BATCH, RANK), F32),
            pltpu.VMEM((BATCH, RANK), BF16),
            pltpu.VMEM((BATCH, RANK), BF16),
            pltpu.VMEM((BATCH, RANK), BF16),
            pltpu.VMEM((BATCH, RANK), BF16),
            pltpu.VMEM((ROWS, BATCH), F32),
            pltpu.VMEM((ROWS, BATCH), F32),
            pltpu.VMEM((DEVICES, 2, ROWS), F32),
            pltpu.VMEM((DEVICES, 1, 128), F32),
            pltpu.VMEM((DEVICES, 1, 128), F32),
            dma((7,)), dma, dma, dma, dma,
            *group_scratch(LOW), *group_scratch(HIGH), *last_scratch(LAST),
        ],
        compiler_params=pltpu.CompilerParams(
            collective_id=0, has_side_effects=True, vmem_limit_bytes=56 << 20
        ),
        name="cholesky",
    )(
        vectors, columns, inverse_factor, diagonal.reshape(1, ROWS), pivots, shell_map.reshape(1, ROWS)
    )
    return relaid, diagonal_out.reshape(ROWS), sums[0, :SHELLS]


def solution(mesh):
    in_specs = (
        P(("pair", "vec"), None),
        P(None, ("pair", "vec"), None),
        P(),
        P(("pair", "vec")),
        P(),
        P(("pair", "vec")),
    )
    out_specs = (P(("pair", "vec"), None), P(("pair", "vec")), P(("pair", "vec")))
    return jax.shard_map(
        on_device, mesh=mesh, in_specs=in_specs, out_specs=out_specs, check_vma=False
    )
```

time: 896 us -> 121 us (0.14)
  waiting for transfers between devices: 749 us -> 0 us
  Pallas kernels: 0 us -> 116 us
  blocking collectives: 60.2 us -> 0 us
  local copies, waits for them, and re-layouts: 30.4 us -> 4.29 us
  matrix products: 20.9 us -> 0 us
  between operations: 19.1 us -> 0.64 us
  other arithmetic: 11.7 us -> 0 us
    psum x2 -> x0, waiting for transfers between devices: 513 us -> none  [from_root(): return lax.psum(jnp.where(mine, shard, jnp.zeros_like(shard)), axis)]
    unnamed x4 -> x0, waiting for transfers between devices: 236 us -> none
    pallas_call x0 -> x1, Pallas kernels: none -> 116 us  [on_device(): pl.pallas_call(kernel, out_shape=[jax.ShapeDtypeStruct((2, ROWS * DEVICES...]
    all_to_all x1 -> x0, blocking collectives: 60.2 us -> none  [on_device(): lax.all_to_all(stacked, 'pair', split_axis=0, concat_axis=1, tiled=True)]
    dot_general x5 -> x0, matrix products: 20.9 us -> none  [contract(): lax.dot_general(left, right, (((left_dim,), (right_dim,)), ((), ())), pre...]
    gather x3 -> x0, local copies, waits for them, and re-layouts: 11.7 us -> none  [the longest x1 5.89 us: on_device(): jnp.take(vectors, local_second, axis=0, mode='clip')]
  transfers between devices with their start and end apart: 4 -> 0, of which waited for: 3 -> 0; matrix products, arithmetic and copies ran while one was open for 2% -> 0% of each run, Pallas kernels for 0% -> 0%
where the time goes in v2:
time: 121 us
  Pallas kernels  116 us (96%)
  local copies, waits for them, and re-layouts  4.29 us (4%)
    pallas_call x1, Pallas kernels, on_device(): pl.pallas_call(kernel, out_shape=[jax.ShapeDtypeStruct((2, ROWS * DEVICES...  116 us
    unnamed x4, local copies, waits for them, and re-layouts  3.21 us

profile of v2, /device:TPU:1, one launch (start us, length us, event | category | flops | bytes accessed | tf_op | source)
XLA Modules:
  0.0 120.9 jit_solution(14126812085217366718)
XLA Ops:
  0.6 116.0 %cholesky.1 = (f32[2,262144]{1,0:T(2,128)}, f32[1,1024]{1,0:T(1,128)}, f32[1,128]{1,0:T(1,128)}) custom-call(f32[1024,1536]{1,0:T(8,128)} %vectors.1, f32[2,1024,256]{2,1,0:T(8,128)} %columns.1, f32[2,256,256]{2,1,0:T(8,128)} %factor.1, f32[1,1024]{1,0:T(1,128)} %bitcast.5, s32[2,256]{1,0:T(2,128)} %pivots.1, s32[1,1024]{1,0:T(1,128)} %bitcast.6), custom_call_target="tpu_custom_call" | custom-call | tf_op jit(solution)/shard_map/cholesky/pallas_call | solution.py:466
  116.6 1.1 slice_bitcast_fusion
  117.7 0.0 copy-start
  117.7 2.6 %copy.11 = f32[2,262144]{1,0:T(2,128)} copy(f32[2,262144]{1,0:T(2,128)} %get-tuple-element.12) | data formatting | bytes 4194304
  120.3 0.0 copy-done
  120.3 0.6 copy.12
Async XLA Ops:
  117.7 2.6 %copy-start = (f32[1,1024]{1,0:T(1,128)S(1)}, f32[1,1024]{1,0:T(1,128)}, u32[]{:S(2)}) copy-start(f32[1,1024]{1,0:T(1,128)} %get-tuple-element.7) | copy-start | bytes 12292

commit v3 on v2

--- a/solution.py
+++ b/solution.py
@@ -22,7 +22,8 @@
 LOW = (0, 512, 128)
 HIGH = (1024, 384, 128)
 WIDE = RANK + BATCH
-LAST = (0, 768, 1536)
+LAST_LOW = (0, 384, 768)
+LAST_HIGH = (768, 384, 768)
 
 
 def split(x):
@@ -75,6 +76,8 @@
 def last_scratch(spec):
     _, width, _ = spec
     return [
+        pltpu.VMEM((32, width), F32),
+        pltpu.VMEM((32, width), F32),
         pltpu.VMEM((8, 2 * width), F32),
         pltpu.SemaphoreType.DMA((12,)),
         pltpu.SemaphoreType.DMA((16,)),
@@ -82,9 +85,9 @@
 
 
 def kernel(
-    vectors, columns, factor, diagonal, pivots, shells,
+    vectors, columns, factors, diagonal, pivots, shells,
     relaid, diagonal_out, sums_out,
-    v32, vh, vl, c32, pick, pick_last, pa, pb, pah, pal, pbh, pbl, ya, yb,
+    v32, vh, vl, c32, factor, pick, pick_last, pa, pb, pah, pal, pbh, pbl, ya, yb,
     new, sums, arrived, load_sem, exchange_send, exchange_recv, sums_send, sums_recv,
     *group_refs,
 ):
@@ -94,7 +97,7 @@
     me = pair * NX + x
     n = len(group_scratch(LOW))
     low, high = Group(LOW, group_refs[:n]), Group(HIGH, group_refs[n : 2 * n])
-    g2_last, last_send, last_recv = group_refs[2 * n :]
+    last_low, last_high = (LAST_LOW, *group_refs[2 * n : 2 * n + 5]), (LAST_HIGH, *group_refs[2 * n + 5 :])
 
     def at(z=z, y=y, x=x, c=c):
         return ((z * NY + y) * NC + c, x)
@@ -126,6 +129,8 @@
         load(i).start()
     load_columns = pltpu.make_async_copy(columns, c32, load_sem.at[6])
     load_columns.start()
+    load_factors = pltpu.make_async_copy(factors, factor, load_sem.at[7])
+    load_factors.start()
 
     barrier = pltpu.get_barrier_semaphore()
 
@@ -139,9 +144,9 @@
     for d in range(1, NZ):
         greet(at(z=along_z(d)))
     root = me == DEVICES - 1
-    apart = (x != NX - 1).astype(jnp.int32) + (y != NY - 1).astype(jnp.int32) + (c != NC - 1).astype(jnp.int32)
-
-    @pl.when((z == NZ - 1) & (apart >= 2))
+    in_last = z == NZ - 1
+
+    @pl.when(in_last & (c != NC - 1) & ((x == NX - 1) != (y == NY - 1)))
     def _():
         greet(at(z=NZ - 1, y=NY - 1, x=NX - 1, c=NC - 1))
 
@@ -281,119 +286,163 @@
 
         spread_sent(pa, width, send)
 
-    def from_last():
-        first, width, _ = LAST
+    def from_last(spec, block_a, block_b, g2, send, recv):
+        first, width, _ = spec
 
         @pl.when(root)
         def _():
-            def rows_of(y, x, c):
-                cols = half(first, width, c)
-                return (
-                    pick_last.at[pl.ds(times(x * NY + y, 8), 8), cols],
-                    pick_last.at[pl.ds(pl.multiple_of(128 + (y * NX + x) * 8, 8), 8), cols],
-                )
-
-            for part, src in enumerate(rows_of(y, x, c)):
-                g2_last[:, part * width : (part + 1) * width] = src[...]
-
-            def send_to(k, carry):
-                y_to, x_to, c_to = (y + k // 2) % NY, (x + k // 8) % NX, (c + k) % NC
-                for part, src in enumerate(rows_of(y_to, x_to, c_to)):
-                    push(src, g2_last.at[:, pl.ds(part * width, width)], last_send.at[0], last_recv.at[0],
-                         at(y=y_to, x=x_to, c=c_to))
-                return carry
-
-            lax.fori_loop(1, NY * NX * NC, send_to, 0)
-
-        yield
-
-        @pl.when((z == NZ - 1) & jnp.logical_not(root))
-        def _():
-            take(g2_last, last_recv.at[0])
-
-        @pl.when(z == NZ - 1)
+            block_a[...] = pick_last[pl.ds(times(x, 32), 32), half(first, width, c)]
+            block_b[...] = pick_last[pl.ds(pl.multiple_of(128 + y * 32, 32), 32), half(first, width, c)]
+            for d in range(4):
+                for core in (c, 1 - c) if d else (1 - c,):
+                    cols = half(first, width, core)
+                    to = along_x(d)
+                    push(pick_last.at[pl.ds(times(to, 32), 32), cols], block_a, send.at[0], recv.at[0], at(x=to, c=core))
+                    to = along_y(d)
+                    push(pick_last.at[pl.ds(pl.multiple_of(128 + to * 32, 32), 32), cols], block_b, send.at[0], recv.at[2], at(y=to, c=core))
+
+        yield
+
+        @pl.when(in_last & (y == NY - 1) & jnp.logical_not(root))
+        def _():
+            take(block_a, recv.at[0])
+
+        @pl.when(in_last & (y == NY - 1))
+        def _():
+            for d in range(1, 4):
+                to = along_y(d)
+                push(block_a.at[pl.ds(times(to, 8), 8)], g2.at[:, pl.ds(0, width)], send.at[2], recv.at[3], at(y=to))
+            g2[:, :width] = block_a[pl.ds(times(y, 8), 8), :]
+
+        @pl.when(in_last & (x == NX - 1) & jnp.logical_not(root))
+        def _():
+            take(block_b, recv.at[2])
+
+        @pl.when(in_last & (x == NX - 1))
+        def _():
+            for d in range(1, 4):
+                to = along_x(d)
+                push(block_b.at[pl.ds(times(to, 8), 8)], g2.at[:, pl.ds(width, width)], send.at[3], recv.at[4], at(x=to))
+            g2[:, width:] = block_b[pl.ds(times(x, 8), 8), :]
+
+        yield
+
+        @pl.when(in_last & (y != NY - 1))
+        def _():
+            take(g2.at[:, pl.ds(0, width)], recv.at[3])
+
+        @pl.when(in_last & (x != NX - 1))
+        def _():
+            take(g2.at[:, pl.ds(width, width)], recv.at[4])
+
+        @pl.when(in_last)
         def _():
             for d in range(1, NZ):
-                push(g2_last, g2_last, last_send.at[1], last_recv.at[1], at(z=along_z(d)))
-
-        yield
-
-        @pl.when(z != NZ - 1)
-        def _():
-            take(g2_last, last_recv.at[1])
-
-        yield from spread(pb, g2_last, first, width, last_send, last_recv)
-
-    def from_last_sent():
-        _, width, _ = LAST
+                push(g2, g2, send.at[1], recv.at[1], at(z=along_z(d)))
+
+        yield
+
+        @pl.when(jnp.logical_not(in_last))
+        def _():
+            take(g2, recv.at[1])
+
+        yield from spread(pb, g2, first, width, send, recv)
+
+    def from_last_sent(spec, block_a, block_b, g2, send, recv):
+        _, width, _ = spec
 
         @pl.when(root)
         def _():
-            take(pick_last.at[pl.ds(0, 248)], last_send.at[0])
-
-        @pl.when(z == NZ - 1)
-        def _():
-            take(pick_last.at[pl.ds(0, 56)], last_send.at[1])
-
-        spread_sent(pb, width, last_send)
-
-    for i in order[:4]:
-        gather(i)
+            take(pick_last.at[pl.ds(0, 224), pl.ds(0, 2 * width)], send.at[0])
+
+        @pl.when(in_last & (y == NY - 1))
+        def _():
+            take(pick_last.at[pl.ds(0, 24), pl.ds(0, width)], send.at[2])
+
+        @pl.when(in_last & (x == NX - 1))
+        def _():
+            take(pick_last.at[pl.ds(0, 24), pl.ds(0, width)], send.at[3])
+
+        @pl.when(in_last)
+        def _():
+            take(pick_last.at[pl.ds(0, 56), pl.ds(0, 2 * width)], send.at[1])
+
+        spread_sent(pb, width, send)
+
+    gather(order[0])
+    gather(order[1])
 
     @pl.when(root)
     def _():
-        pl.semaphore_wait(barrier, 38)
+        pl.semaphore_wait(barrier, 20)
 
     @pl.when(jnp.logical_not(root))
     def _():
         pl.semaphore_wait(barrier, 14)
 
-    a, b, last = reduce(low), reduce(high), from_last()
+    a, b = reduce(low), reduce(high)
+    p, q = from_last(*last_low), from_last(*last_high)
 
     def go(*streams):
         for stream in streams:
             next(stream, None)
 
+    def times_last(i):
+        rows = pl.ds(i * 256, 256)
+        yb[rows, :] = three(dot_nt, (vh[rows, :], vl[rows, :]), (pbh[...], pbl[...]))
+
+    def times_other(i, cols):
+        rows = pl.ds(i * 256, 256)
+        return three(dot_nt, (vh[rows, cols], vl[rows, cols]), (pah[:, cols], pal[:, cols]))
+
     go(a)
+    gather(order[2])
+    gather(order[3])
+    go(p, a)
     gather(order[4])
     gather(order[5])
     load_columns.wait()
+    load_factors.wait()
     own = split(c32[0])
     pick[:, RANK:] = dot_nn(hot_second, own[0]) + dot_nn(hot_second, own[1])
-    go(b, last)
-    go(a, b, a, b, last, a, b, last, a, b, last, a, b, last, a, b, last)
-
-    pbh[...], pbl[...] = split(pb[...])
-
-    def times_last(i, carry):
-        rows = pl.ds(times(i, 256), 256)
-        yb[rows, :] = three(dot_nt, (vh[rows, :], vl[rows, :]), (pbh[...], pbl[...]))
-        return carry
-
-    lax.fori_loop(0, ROWS // 256, times_last, 0)
-    go(a, b, a, b)
-
+    go(b, q, b, p, a, q, b, p, a, q, b, a, p, b, q, a, p, b, q, a, b, p, q, p)
+    low_cols, high_cols = pl.ds(0, RANK // 2), pl.ds(RANK // 2, RANK // 2)
+    pbh[:, low_cols], pbl[:, low_cols] = split(pb[:, low_cols])
+    go(a, q)
+    pbh[:, high_cols], pbl[:, high_cols] = split(pb[:, high_cols])
+    times_last(0)
+    times_last(1)
+    go(b)
+    times_last(2)
+    times_last(3)
+
+    low_cols, high_cols = pl.ds(0, HIGH[0]), pl.ds(HIGH[0], RANK - HIGH[0])
     f0, f1 = factor[0], factor[1]
-    pah[...], pal[...] = split(pa[:, :RANK])
-    cross = three(dot_nt, (pah[...], pal[...]), (pbh[...], pbl[...]))
+    f0_parts = split(f0)
+    f0_t, f1_t = split(f0.T), split(f1.T)
+
+    def cross_part(cols):
+        return three(dot_nt, (pah[:, cols], pal[:, cols]), (pbh[:, cols], pbl[:, cols]))
+
+    go(a)
+    pah[:, low_cols], pal[:, low_cols] = split(pa[:, low_cols])
+    for i in range(ROWS // 256):
+        ya[pl.ds(i * 256, 256), :] = times_other(i, low_cols)
+    cross = cross_part(low_cols)
+    go(b)
+    pah[:, high_cols], pal[:, high_cols] = split(pa[:, high_cols])
+    cross = cross + cross_part(high_cols)
     last_first = jnp.broadcast_to(pivots[0:1, 0:1], (BATCH, BATCH)) >= (DEVICES - 1) * ROWS
     cross = jnp.where(last_first, cross, cross.T)
-    f0_parts = split(f0)
     pivot_new = three(dot_nn, split(pa[:, RANK:] - cross), f0_parts)
     onto = split(three(dot_nt, f0_parts, split(pivot_new)))
-    f0_t, f1_t = split(f0.T), split(f1.T)
     last_first = jnp.broadcast_to(pivots[0:1, 0:1], (BLOCK, BATCH)) >= (DEVICES - 1) * ROWS
-
-    def times_other(i, carry):
-        rows = pl.ds(times(i, 256), 256)
-        ya[rows, :] = three(dot_nt, (vh[rows, :], vl[rows, :]), (pah[...], pal[...]))
-        return carry
-
-    lax.fori_loop(0, ROWS // 256, times_other, 0)
 
     kinds = DEVICES // 2
     for block in range(ROWS // BLOCK):
         rows = pl.ds(block * BLOCK, BLOCK)
+        for i in range(block * BLOCK // 256, (block + 1) * BLOCK // 256):
+            ya[pl.ds(i * 256, 256), :] += times_other(i, high_cols)
         y_a, y_b = ya[rows, :], yb[rows, :]
         resid = c32[0, rows, :] - jnp.where(last_first, y_b, y_a)
         parts = split(resid)
@@ -451,9 +500,10 @@
 
     reduce_sent(low)
     reduce_sent(high)
-    from_last_sent()
+    from_last_sent(*last_low)
+    from_last_sent(*last_high)
     take(arrived, sums_recv)
-    sums_out[...] = jnp.sum(arrived[...], axis=0)
+    sums_out[...] = jnp.sum(arrived[...], axis=0)[:, :SHELLS]
     take(relaid, exchange_recv)
     take(new.at[pl.ds(0, DEVICES - 1)], exchange_send)
     take(sums.at[pl.ds(0, DEVICES - 1)], sums_send)
@@ -461,22 +511,23 @@
 
 def on_device(vectors, columns, inverse_factor, diagonal, pivots, shell_map):
     vmem = pl.BlockSpec(memory_space=pltpu.VMEM)
-    hbm = pl.BlockSpec(memory_space=pl.ANY)
+    hbm = pl.BlockSpec(memory_space=pltpu.HBM)
     dma = pltpu.SemaphoreType.DMA
     relaid, diagonal_out, sums = pl.pallas_call(
         kernel,
         out_shape=[
             jax.ShapeDtypeStruct((2, ROWS * DEVICES), F32),
             jax.ShapeDtypeStruct((1, ROWS), F32),
-            jax.ShapeDtypeStruct((1, 128), F32),
+            jax.ShapeDtypeStruct((1, SHELLS), F32),
         ],
-        in_specs=[hbm, hbm, vmem, vmem, vmem, vmem],
-        out_specs=[hbm, vmem, vmem],
+        in_specs=[hbm, hbm, hbm, vmem, vmem, vmem],
+        out_specs=[pl.BlockSpec(memory_space=pl.ANY), vmem, vmem],
         scratch_shapes=[
             pltpu.VMEM((ROWS, RANK), F32),
             pltpu.VMEM((ROWS, RANK), BF16),
             pltpu.VMEM((ROWS, RANK), BF16),
             pltpu.VMEM((2, ROWS, BATCH), F32),
+            pltpu.VMEM((2, BATCH, BATCH), F32),
             pltpu.VMEM((BATCH, WIDE), F32),
             pltpu.VMEM((BATCH, RANK), F32),
             pltpu.VMEM((BATCH, WIDE), F32),
@@ -490,17 +541,17 @@
             pltpu.VMEM((DEVICES, 2, ROWS), F32),
             pltpu.VMEM((DEVICES, 1, 128), F32),
             pltpu.VMEM((DEVICES, 1, 128), F32),
-            dma((7,)), dma, dma, dma, dma,
-            *group_scratch(LOW), *group_scratch(HIGH), *last_scratch(LAST),
+            dma((8,)), dma, dma, dma, dma,
+            *group_scratch(LOW), *group_scratch(HIGH), *last_scratch(LAST_LOW), *last_scratch(LAST_HIGH),
         ],
         compiler_params=pltpu.CompilerParams(
-            collective_id=0, has_side_effects=True, vmem_limit_bytes=56 << 20
+            collective_id=0, has_side_effects=True, vmem_limit_bytes=60 << 20
         ),
         name="cholesky",
     )(
         vectors, columns, inverse_factor, diagonal.reshape(1, ROWS), pivots, shell_map.reshape(1, ROWS)
     )
-    return relaid, diagonal_out.reshape(ROWS), sums[0, :SHELLS]
+    return relaid, diagonal_out.reshape(ROWS), sums.reshape(SHELLS)
 
 
 def solution(mesh):

time: 121 us -> 113 us (0.934)
  Pallas kernels: 116 us -> 109 us
    pallas_call x1, Pallas kernels: 116 us -> 109 us  [on_device(): pl.pallas_call(kernel, out_shape=[jax.ShapeDtypeStruct((2, ROWS * DEVICES...]
    unnamed x4 -> x7, local copies, waits for them, and re-layouts: 3.21 us -> 3.73 us
where the time goes in v3:
time: 113 us
  Pallas kernels  109 us (96%)
  local copies, waits for them, and re-layouts  3.73 us (3%)
    pallas_call x1, Pallas kernels, on_device(): pl.pallas_call(kernel, out_shape=[jax.ShapeDtypeStruct((2, ROWS * DEVICES...  109 us
    unnamed x7, local copies, waits for them, and re-layouts  3.73 us

profile of v3, /device:TPU:1, one launch (start us, length us, event | category | flops | bytes accessed | tf_op | source)
XLA Modules:
  0.0 113.1 jit_solution(8674824376996063519)
XLA Ops:
  0.6 108.7 %cholesky.1 = (f32[2,262144]{1,0:T(2,128)}, f32[1,1024]{1,0:T(1,128)}, f32[1,64]{1,0:T(1,128)}) custom-call(f32[1024,1536]{1,0:T(8,128)} %vectors.1, f32[2,1024,256]{2,1,0:T(8,128)} %columns.1, f32[2,256,256]{2,1,0:T(8,128)} %factors.1, f32[1,1024]{1,0:T(1,128)} %bitcast.4, s32[2,256]{1,0:T(2,128)} %pivots.1, s32[1,1024]{1,0:T(1,128)} %bitcast.5), custom_call_target="tpu_custom_call" | custom-call | tf_op jit(solution)/shard_map/cholesky/pallas_call | solution.py:516
  109.4 0.0 copy-start
  109.4 0.0 copy-start.1
  109.4 2.6 %copy.12 = f32[2,262144]{1,0:T(2,128)} copy(f32[2,262144]{1,0:T(2,128)} %get-tuple-element.12) | data formatting | bytes 4194304
  112.0 0.0 copy-done
  112.0 0.6 copy.13
  112.6 0.0 copy-done.1
  112.6 0.5 copy.14
Async XLA Ops:
  109.4 2.6 %copy-start = (f32[1,1024]{1,0:T(1,128)S(1)}, f32[1,1024]{1,0:T(1,128)}, u32[]{:S(2)}) copy-start(f32[1,1024]{1,0:T(1,128)} %get-tuple-element.7) | copy-start | bytes 12292
  109.4 3.2 %copy-start.1 = (f32[1,64]{1,0:T(1,128)S(1)}, f32[1,64]{1,0:T(1,128)}, u32[]{:S(2)}) copy-start(f32[1,64]{1,0:T(1,128)} %get-tuple-element.8) | copy-start | bytes 772

commit v4 on v3

--- a/solution.py
+++ b/solution.py
@@ -17,7 +17,7 @@
 ROWS = 1024
 DEVICES = NZ * NY * NX * NC
 SHELLS = 64
-BLOCK = 512
+BLOCKS = ((0, 256), (256, 256), (512, 512))
 
 LOW = (0, 512, 128)
 HIGH = (1024, 384, 128)
@@ -88,7 +88,8 @@
     vectors, columns, factors, diagonal, pivots, shells,
     relaid, diagonal_out, sums_out,
     v32, vh, vl, c32, factor, pick, pick_last, pa, pb, pah, pal, pbh, pbl, ya, yb,
-    new, sums, arrived, load_sem, exchange_send, exchange_recv, sums_send, sums_recv,
+    new, sums, sums_y, sums_plane, sums_z, part_y, part_plane,
+    load_sem, exchange_send, exchange_recv, sums_send, sums_recv,
     *group_refs,
 ):
     pair = lax.axis_index("pair")
@@ -369,8 +370,8 @@
 
         spread_sent(pb, width, send)
 
-    gather(order[0])
-    gather(order[1])
+    for i in order[:5]:
+        gather(i)
 
     @pl.when(root)
     def _():
@@ -391,21 +392,17 @@
         rows = pl.ds(i * 256, 256)
         yb[rows, :] = three(dot_nt, (vh[rows, :], vl[rows, :]), (pbh[...], pbl[...]))
 
-    def times_other(i, cols):
+    def times_other(i):
         rows = pl.ds(i * 256, 256)
-        return three(dot_nt, (vh[rows, cols], vl[rows, cols]), (pah[:, cols], pal[:, cols]))
-
-    go(a)
-    gather(order[2])
-    gather(order[3])
-    go(p, a)
-    gather(order[4])
+        return three(dot_nt, (vh[rows, :], vl[rows, :]), (pah[...], pal[...]))
+
+    go(a, p)
     gather(order[5])
     load_columns.wait()
     load_factors.wait()
     own = split(c32[0])
     pick[:, RANK:] = dot_nn(hot_second, own[0]) + dot_nn(hot_second, own[1])
-    go(b, q, b, p, a, q, b, p, a, q, b, a, p, b, q, a, p, b, q, a, b, p, q, p)
+    go(b, a, q, b, p, a, q, b, p, a, q, b, a, p, b, q, a, p, b, q, a, b, p, q, p)
     low_cols, high_cols = pl.ds(0, RANK // 2), pl.ds(RANK // 2, RANK // 2)
     pbh[:, low_cols], pbl[:, low_cols] = split(pb[:, low_cols])
     go(a, q)
@@ -426,8 +423,6 @@
 
     go(a)
     pah[:, low_cols], pal[:, low_cols] = split(pa[:, low_cols])
-    for i in range(ROWS // 256):
-        ya[pl.ds(i * 256, 256), :] = times_other(i, low_cols)
     cross = cross_part(low_cols)
     go(b)
     pah[:, high_cols], pal[:, high_cols] = split(pa[:, high_cols])
@@ -436,77 +431,119 @@
     cross = jnp.where(last_first, cross, cross.T)
     pivot_new = three(dot_nn, split(pa[:, RANK:] - cross), f0_parts)
     onto = split(three(dot_nt, f0_parts, split(pivot_new)))
-    last_first = jnp.broadcast_to(pivots[0:1, 0:1], (BLOCK, BATCH)) >= (DEVICES - 1) * ROWS
 
     kinds = DEVICES // 2
-    for block in range(ROWS // BLOCK):
-        rows = pl.ds(block * BLOCK, BLOCK)
-        for i in range(block * BLOCK // 256, (block + 1) * BLOCK // 256):
-            ya[pl.ds(i * 256, 256), :] += times_other(i, high_cols)
+    half_z = [lax.rem(z + i, NZ // 2) for i in range(NZ // 2)]
+
+    def rest_of(k):
+        y_to = lax.rem(y + lax.rem(k, NY), NY)
+        x_to = lax.rem(x + lax.rem(lax.div(k, NY), NX), NX)
+        c_to = lax.rem(c + lax.div(k, NY * NX), NC)
+        return y_to * NC + c_to, x_to
+
+    def shell_steps():
+        shell = shells[...]
+        device = shell // SHELLS
+        place = (device % (NY * NX * NC)) * NZ + device // (NY * NX * NC)
+        hot_device = jnp.where(
+            lax.broadcasted_iota(jnp.int32, (DEVICES, ROWS), 0) == place, 1.0, 0.0
+        ).astype(BF16)
+        values = jnp.where(
+            lax.broadcasted_iota(jnp.int32, (128, ROWS), 0) == shell % SHELLS, diagonal_out[...], 0.0
+        )
+        first = values.astype(BF16)
+        second, third = split(values - first.astype(F32))
+        sums[...] = dot_nt(hot_device, first) + (dot_nt(hot_device, second) + dot_nt(hot_device, third))
+        for d in range(1, NY):
+            to = along_y(d)
+            push(sums.at[pl.ds(times(to, 64), 64)], sums_y.at[d - 1], sums_send.at[0], sums_recv.at[0], at(y=to))
+        yield
+        take(sums_y, sums_recv.at[0])
+        part_y[...] = (sums[pl.ds(times(y, 64), 64), :] + sums_y[0]) + (sums_y[1] + sums_y[2])
+        for d in range(1, NX * NC):
+            x_to, c_to = along_x(d % NX), lax.rem(c + d // NX, NC)
+            push(part_y.at[pl.ds(times(c_to * NX + x_to, 8), 8)], sums_plane.at[d - 1], sums_send.at[1], sums_recv.at[1], at(x=x_to, c=c_to))
+        yield
+        take(sums_plane, sums_recv.at[1])
+        total = part_y[pl.ds(times(c * NX + x, 8), 8), :]
+        for d in range(1, NX * NC):
+            total = total + sums_plane[d - 1]
+        part_plane[...] = total
+        for d in range(1, NZ):
+            push(part_plane, sums_z.at[d - 1], sums_send.at[2], sums_recv.at[2], at(z=along_z(d)))
+        yield
+        take(sums_z, sums_recv.at[2])
+        total = part_plane[pl.ds(z, 1), :]
+        for d in range(1, NZ):
+            total = total + sums_z[d - 1, pl.ds(z, 1), :]
+        sums_out[...] = total[:, :SHELLS]
+
+    shell = shell_steps()
+    for start, count in BLOCKS:
+        rows = pl.ds(start, count)
+        for i in range(start // 256, (start + count) // 256):
+            ya[pl.ds(i * 256, 256), :] = times_other(i)
         y_a, y_b = ya[rows, :], yb[rows, :]
+        last_first = jnp.broadcast_to(pivots[0:1, 0:1], (count, BATCH)) >= (DEVICES - 1) * ROWS
         resid = c32[0, rows, :] - jnp.where(last_first, y_b, y_a)
         parts = split(resid)
         new_first = three(dot_nt, f0_t, parts)
         resid = c32[1, rows, :] - jnp.where(last_first, y_a, y_b) - three(dot_nn, parts, onto)
         new_second = three(dot_nt, f1_t, split(resid))
-        new[:kinds, :, rows] = new_first.reshape(kinds, 2, BLOCK)
-        new[kinds:, :, rows] = new_second.reshape(kinds, 2, BLOCK)
+        new[:kinds, :, rows] = new_first.reshape(kinds, 2, count)
+        new[kinds:, :, rows] = new_second.reshape(kinds, 2, count)
         diagonal_out[:, rows] = diagonal[:, rows] - jnp.sum(
             new_first * new_first + new_second * new_second, axis=0, keepdims=True
         )
-        here = relaid.at[:, pl.ds(pl.multiple_of(me * ROWS + block * BLOCK, BLOCK), BLOCK)]
+        here = relaid.at[:, pl.ds(pl.multiple_of(me * ROWS + start, 256), count)]
+
+        is_last = start + count == ROWS
+        if is_last:
+            go(shell)
 
         def send_new(k, carry):
-            y_to, x_to, c_to = (y + k // 4) % NY, (x + k // 16) % NX, (c + k // 64) % NC
+            pair_rest, x_to = rest_of(k)
+            for i in range(NZ // 2):
+                for batch in range(2):
+                    pair_to = (batch * (NZ // 2) + half_z[i]) * (NY * NC) + pair_rest
+                    push(new.at[pair_to * NX + x_to, :, rows], here, exchange_send, exchange_recv, (pair_to, x_to))
+            return carry
+
+        for i in range(NZ // 2):
             for batch in range(2):
-                z_to = batch * (NZ // 2) + (z + k) % (NZ // 2)
-                pair_to, x_to = at(z=z_to, y=y_to, x=x_to, c=c_to)
-                to = pair_to * NX + x_to
-                src = new.at[to, :, rows]
-
-                @pl.when(to == me)
-                def _():
-                    pltpu.make_async_copy(src, here, exchange_recv).start()
-
-                @pl.when(to != me)
-                def _():
-                    push(src, here, exchange_send, exchange_recv, (pair_to, x_to))
-
-            return carry
-
-        lax.fori_loop(0, kinds, send_new, 0)
-
-    shell = shells[...]
-    hot_device = jnp.where(
-        lax.broadcasted_iota(jnp.int32, (DEVICES, ROWS), 0) == shell // SHELLS, 1.0, 0.0
-    ).astype(BF16)
-    values = jnp.where(
-        lax.broadcasted_iota(jnp.int32, (128, ROWS), 0) == shell % SHELLS, diagonal_out[...], 0.0
-    )
-    first, rest = values.astype(BF16), values
-    rest = rest - first.astype(F32)
-    second, third = split(rest)
-    total = dot_nt(hot_device, first) + (dot_nt(hot_device, second) + dot_nt(hot_device, third))
-    sums[...] = total.reshape(DEVICES, 1, 128)
-    pltpu.make_async_copy(sums.at[me], arrived.at[me], sums_recv).start()
-
-    def send_sums(k, carry):
-        z_to, y_to, x_to, c_to = along_z(k), (y + k // 8) % NY, (x + k // 32) % NX, (c + k // 128) % NC
-        pair_to, x_to = at(z=z_to, y=y_to, x=x_to, c=c_to)
-        push(sums.at[pair_to * NX + x_to], arrived.at[me], sums_send, sums_recv, (pair_to, x_to))
-        return carry
-
-    lax.fori_loop(1, DEVICES, send_sums, 0)
+                z_to = batch * (NZ // 2) + half_z[i]
+                src = new.at[at(z=z_to)[0] * NX + x, :, rows]
+                if i:
+                    push(src, here, exchange_send, exchange_recv, at(z=z_to))
+                else:
+
+                    @pl.when(z_to == z)
+                    def _():
+                        pltpu.make_async_copy(src, here, exchange_recv).start()
+
+                    @pl.when(z_to != z)
+                    def _():
+                        push(src, here, exchange_send, exchange_recv, at(z=z_to))
+
+        places = NY * NX * NC
+        if is_last:
+            for a, b in ((1, 11), (11, 21), (21, places)):
+                lax.fori_loop(a, b, send_new, 0)
+                if b < places:
+                    go(shell)
+        else:
+            lax.fori_loop(1, places, send_new, 0)
 
     reduce_sent(low)
     reduce_sent(high)
     from_last_sent(*last_low)
     from_last_sent(*last_high)
-    take(arrived, sums_recv)
-    sums_out[...] = jnp.sum(arrived[...], axis=0)[:, :SHELLS]
+    go(shell)
     take(relaid, exchange_recv)
     take(new.at[pl.ds(0, DEVICES - 1)], exchange_send)
-    take(sums.at[pl.ds(0, DEVICES - 1)], sums_send)
+    take(sums_y, sums_send.at[0])
+    take(sums_plane, sums_send.at[1])
+    take(sums_z, sums_send.at[2])
 
 
 def on_device(vectors, columns, inverse_factor, diagonal, pivots, shell_map):
@@ -539,9 +576,13 @@
             pltpu.VMEM((ROWS, BATCH), F32),
             pltpu.VMEM((ROWS, BATCH), F32),
             pltpu.VMEM((DEVICES, 2, ROWS), F32),
-            pltpu.VMEM((DEVICES, 1, 128), F32),
-            pltpu.VMEM((DEVICES, 1, 128), F32),
-            dma((8,)), dma, dma, dma, dma,
+            pltpu.VMEM((DEVICES, 128), F32),
+            pltpu.VMEM((NY - 1, 64, 128), F32),
+            pltpu.VMEM((NX * NC - 1, 8, 128), F32),
+            pltpu.VMEM((NZ - 1, 8, 128), F32),
+            pltpu.VMEM((64, 128), F32),
+            pltpu.VMEM((8, 128), F32),
+            dma((8,)), dma, dma, dma((3,)), dma((3,)),
             *group_scratch(LOW), *group_scratch(HIGH), *last_scratch(LAST_LOW), *last_scratch(LAST_HIGH),
         ],
         compiler_params=pltpu.CompilerParams(

time: 113 us -> 109 us (0.965)
  Pallas kernels: 109 us -> 105 us
    pallas_call x1, Pallas kernels: 109 us -> 105 us  [on_device(): pl.pallas_call(kernel, out_shape=[jax.ShapeDtypeStruct((2, ROWS * DEVICES...]
where the time goes in v4:
time: 109 us
  Pallas kernels  105 us (96%)
  local copies, waits for them, and re-layouts  3.73 us (3%)
    pallas_call x1, Pallas kernels, on_device(): pl.pallas_call(kernel, out_shape=[jax.ShapeDtypeStruct((2, ROWS * DEVICES...  105 us
    unnamed x7, local copies, waits for them, and re-layouts  3.73 us

profile of v4, /device:TPU:1, one launch (start us, length us, event | category | flops | bytes accessed | tf_op | source)
XLA Modules:
  0.0 108.9 jit_solution(1225138716258682020)
XLA Ops:
  0.6 104.5 %cholesky.1 = (f32[2,262144]{1,0:T(2,128)}, f32[1,1024]{1,0:T(1,128)}, f32[1,64]{1,0:T(1,128)}) custom-call(f32[1024,1536]{1,0:T(8,128)} %vectors.1, f32[2,1024,256]{2,1,0:T(8,128)} %columns.1, f32[2,256,256]{2,1,0:T(8,128)} %factors.1, f32[1,1024]{1,0:T(1,128)} %bitcast.4, s32[2,256]{1,0:T(2,128)} %pivots.1, s32[1,1024]{1,0:T(1,128)} %bitcast.5), custom_call_target="tpu_custom_call" | custom-call | tf_op jit(solution)/shard_map/cholesky/pallas_call | solution.py:553
  105.2 0.0 copy-start
  105.2 0.0 copy-start.1
  105.2 2.6 %copy.12 = f32[2,262144]{1,0:T(2,128)} copy(f32[2,262144]{1,0:T(2,128)} %get-tuple-element.12) | data formatting | bytes 4194304
  107.8 0.0 copy-done
  107.8 0.6 copy.13
  108.4 0.0 copy-done.1
  108.4 0.5 copy.14
Async XLA Ops:
  105.2 2.6 %copy-start = (f32[1,1024]{1,0:T(1,128)S(1)}, f32[1,1024]{1,0:T(1,128)}, u32[]{:S(2)}) copy-start(f32[1,1024]{1,0:T(1,128)} %get-tuple-element.7) | copy-start | bytes 12292
  105.2 3.2 %copy-start.1 = (f32[1,64]{1,0:T(1,128)S(1)}, f32[1,64]{1,0:T(1,128)}, u32[]{:S(2)}) copy-start(f32[1,64]{1,0:T(1,128)} %get-tuple-element.8) | copy-start | bytes 772

commit v5 on v4

--- a/solution.py
+++ b/solution.py
@@ -17,7 +17,7 @@
 ROWS = 1024
 DEVICES = NZ * NY * NX * NC
 SHELLS = 64
-BLOCKS = ((0, 256), (256, 256), (512, 512))
+BLOCKS = ((0, 512), (512, 512))
 
 LOW = (0, 512, 128)
 HIGH = (1024, 384, 128)
@@ -408,10 +408,9 @@
     go(a, q)
     pbh[:, high_cols], pbl[:, high_cols] = split(pb[:, high_cols])
     times_last(0)
-    times_last(1)
     go(b)
-    times_last(2)
-    times_last(3)
+    for i in range(1, BLOCKS[0][1] // 256):
+        times_last(i)
 
     low_cols, high_cols = pl.ds(0, HIGH[0]), pl.ds(HIGH[0], RANK - HIGH[0])
     f0, f1 = factor[0], factor[1]
@@ -482,6 +481,8 @@
     for start, count in BLOCKS:
         rows = pl.ds(start, count)
         for i in range(start // 256, (start + count) // 256):
+            if start:
+                times_last(i)
             ya[pl.ds(i * 256, 256), :] = times_other(i)
         y_a, y_b = ya[rows, :], yb[rows, :]
         last_first = jnp.broadcast_to(pivots[0:1, 0:1], (count, BATCH)) >= (DEVICES - 1) * ROWS

time: 109 us -> 109 us (level)
  no operation moved by 1% of the time
where the time goes in v5:
time: 109 us
  Pallas kernels  105 us (96%)
  local copies, waits for them, and re-layouts  3.73 us (3%)
    pallas_call x1, Pallas kernels, on_device(): pl.pallas_call(kernel, out_shape=[jax.ShapeDtypeStruct((2, ROWS * DEVICES...  105 us
    unnamed x7, local copies, waits for them, and re-layouts  3.73 us

profile of v5, /device:TPU:1, one launch (start us, length us, event | category | flops | bytes accessed | tf_op | source)
XLA Modules:
  0.0 109.0 jit_solution(6104918207901446009)
XLA Ops:
  0.6 104.6 %cholesky.1 = (f32[2,262144]{1,0:T(2,128)}, f32[1,1024]{1,0:T(1,128)}, f32[1,64]{1,0:T(1,128)}) custom-call(f32[1024,1536]{1,0:T(8,128)} %vectors.1, f32[2,1024,256]{2,1,0:T(8,128)} %columns.1, f32[2,256,256]{2,1,0:T(8,128)} %factors.1, f32[1,1024]{1,0:T(1,128)} %bitcast.4, s32[2,256]{1,0:T(2,128)} %pivots.1, s32[1,1024]{1,0:T(1,128)} %bitcast.5), custom_call_target="tpu_custom_call" | custom-call | tf_op jit(solution)/shard_map/cholesky/pallas_call | solution.py:554
  105.3 0.0 copy-start
  105.3 0.0 copy-start.1
  105.3 2.6 %copy.12 = f32[2,262144]{1,0:T(2,128)} copy(f32[2,262144]{1,0:T(2,128)} %get-tuple-element.12) | data formatting | bytes 4194304
  107.9 0.0 copy-done
  107.9 0.6 copy.13
  108.5 0.0 copy-done.1
  108.5 0.5 copy.14
Async XLA Ops:
  105.3 2.6 %copy-start = (f32[1,1024]{1,0:T(1,128)S(1)}, f32[1,1024]{1,0:T(1,128)}, u32[]{:S(2)}) copy-start(f32[1,1024]{1,0:T(1,128)} %get-tuple-element.7) | copy-start | bytes 12292
  105.3 3.2 %copy-start.1 = (f32[1,64]{1,0:T(1,128)S(1)}, f32[1,64]{1,0:T(1,128)}, u32[]{:S(2)}) copy-start(f32[1,64]{1,0:T(1,128)} %get-tuple-element.8) | copy-start | bytes 772
